TPU v7x, 256 devices: a whole 4x4x8 slice. The times are simulated.
256 devices in a mesh: tm: 8 (over z_lo, core), height: 32 (over x, y, z_hi).
Axes of the slice: x: 4, y: 4, z: 8 (z_hi: 2, z_lo: 4; z = z_hi * 4 + z_lo), core: 2. Of those that a mesh axis runs over, the one named last changes fastest.
Arguments:
- clean_latents: bfloat16 [32, 128, 16, 3072], P('tm', 'height'), may hold values from -6 to 6
- gaussian_noise: bfloat16 [32, 128, 16, 3072], P('tm', 'height'), may hold values from -6 to 6
- text_states: bfloat16 [256, 3072], replicated, may hold values from -6 to 6
- queries: bfloat16 [32, 128, 16, 1536], P('tm', 'height'), may hold values from -40 to 40
- key_states: bfloat16 [32, 128, 16, 1536], P('tm', 'height'), may hold values from -8 to 8
- cotangent: bfloat16 [32, 128, 16, 1536], P('tm', 'height'), may hold values from -240 to 240
- text_keys: bfloat16 [256, 1536], replicated, may hold values from -6 to 6
- window_radii: int32 [12, 3], replicated, may hold values from 0 to 1
- timestep: int32 [1], replicated, may hold values from 200 to 799
- sketch_seed: int32 [1], replicated, may hold values from 0 to 65535
- down_image: bfloat16 [3072, 16], replicated, may hold values from -0.109375 to 0.109375
- up_image: bfloat16 [16, 1536], replicated, may hold values from -1.5 to 1.5
- down_text: bfloat16 [3072, 16], replicated, may hold values from -0.109375 to 0.109375
- up_text: bfloat16 [16, 1536], replicated, may hold values from -1.5 to 1.5
Outputs:
- value_grad: bfloat16 [32, 128, 16, 1536], P('tm', 'height')
- grad_sketch: float32 [16384], replicated
All inputs are finite; a program needn't handle non-finite values.
Results may differ from a plain program's by a relative error of at most 0.0075.
Values may be sent and summed in bfloat16 or wider, within the bound.
A program may use at most 128 MiB of HBM per device.

v0:
```python
import jax
import jax.numpy as jnp
from jax import lax
from jax.sharding import PartitionSpec as P

SKETCH = 16384
TW = 8


def padded_2(block, sides, width):
    for axis, dim in sides:
        count = lax.axis_size(axis)
        forward = [(i, i + 1) for i in range(count - 1)]
        backward = [(target, source) for source, target in forward]
        low = lax.ppermute(
            lax.slice_in_dim(block, block.shape[dim] - width, None, axis=dim), axis, forward
        )
        high = lax.ppermute(lax.slice_in_dim(block, 0, width, axis=dim), axis, backward)
        block = jnp.concatenate([low, block, high], axis=dim)
    return block


def shifted(array, axis, by):
    size = lax.axis_size(axis)
    pairs = [(i, i + by) for i in range(size) if 0 <= i + by < size]
    return lax.ppermute(array, axis, pairs)


def tile_rows(block, width):
    frame_count, row_count, col_count = (block.shape[0], block.shape[1], block.shape[2])
    rest = block.shape[3:]
    col_tiles = col_count // width
    shaped = block.reshape((frame_count, row_count, col_tiles, width) + rest)
    order = (2, 0, 1, 3) + tuple(range(4, 4 + len(rest)))
    return jnp.transpose(shaped, order).reshape((col_tiles, frame_count * row_count * width) + rest)


def region_rows(padded, width):
    col_count = padded.shape[2] - 2 * width
    views = [
        tile_rows(padded[:, :, shift_col * width : shift_col * width + col_count], width)
        for shift_col in range(3)
    ]
    return jnp.concatenate(views, axis=1)


def window_mask(
    radius, frame_tile, row_tile, frame_tiles, row_tiles, col_tiles, frame_count, row_count, width
):
    region = 27 * frame_count * row_count * width
    position = jnp.arange(region, dtype=jnp.int32)
    col_step = position // (9 * frame_count * row_count * width) - 1
    frame_step = position // (3 * row_count * width) % (3 * frame_count) // frame_count - 1
    row_step = position // width % (3 * row_count) // row_count - 1
    inside = (
        (jnp.abs(frame_step) <= radius[0])
        & (jnp.abs(row_step) <= radius[1])
        & (jnp.abs(col_step) <= radius[2])
    )
    inside = inside & (frame_tile + frame_step >= 0) & (frame_tile + frame_step < frame_tiles)
    inside = inside & (row_tile + row_step >= 0) & (row_tile + row_step < row_tiles)
    col_index = jnp.arange(col_tiles, dtype=jnp.int32)[:, None]
    return (
        inside[None, :]
        & (col_index + col_step[None, :] >= 0)
        & (col_index + col_step[None, :] < col_tiles)
    )


def forward_head(query_head, key_region, text_head, cot_head, allowed, score_scale):
    image_scores = (
        jnp.einsum("cqd,cld->cql", query_head, key_region, preferred_element_type=jnp.float32)
        * score_scale
    )
    image_scores = jnp.where(allowed[:, None, :], image_scores, -jnp.inf)
    text_scores = (
        jnp.einsum("cqd,td->cqt", query_head, text_head, preferred_element_type=jnp.float32)
        * score_scale
    )
    row_max = jnp.maximum(jnp.max(image_scores, axis=-1), jnp.max(text_scores, axis=-1))
    total = jnp.sum(jnp.exp(image_scores - row_max[..., None]), axis=-1) + jnp.sum(
        jnp.exp(text_scores - row_max[..., None]), axis=-1
    )
    log_total = row_max + jnp.log(total)
    text_probs = jnp.exp(text_scores - log_total[..., None]).astype(jnp.bfloat16)
    text_part = jnp.einsum("cqt,cqd->td", text_probs, cot_head, preferred_element_type=jnp.float32)
    return (image_scores, log_total, text_part)


def place_back(spread, frame_count, row_count, width):
    col_tiles, head_width = (spread.shape[0], spread.shape[2])
    shaped = spread.reshape(col_tiles, 3, 3 * frame_count, 3 * row_count, width, head_width)
    placed = jnp.zeros((3 * frame_count, 3 * row_count, col_tiles, width, head_width), jnp.float32)
    for shift_col in range(3):
        moved = jnp.transpose(shaped[:, shift_col], (1, 2, 0, 3, 4))
        moved = jnp.pad(moved, ((0, 0), (0, 0), (1, 1), (0, 0), (0, 0)))
        placed = placed + moved[:, :, 2 - shift_col : 2 - shift_col + col_tiles]
    return placed.reshape(3 * frame_count, 3 * row_count, col_tiles * width, head_width)


def sketch_signs(seed_value, rows, width):
    row_part = jnp.arange(rows, dtype=jnp.int32)[:, None] * width
    position = row_part + jnp.arange(width, dtype=jnp.int32)[None, :]
    mixed_bits = position * 1103515245 + seed_value * 12345 + 1013904223
    mixed_bits = mixed_bits ^ mixed_bits >> 16
    mixed_bits = mixed_bits * 73244475
    mixed_bits = mixed_bits ^ mixed_bits >> 16
    return (1 - 2 * (mixed_bits >> 7 & 1)).astype(jnp.float32)


def count_sketch(pieces, seed_value, width, sketch_scale):
    flat = jnp.concatenate([piece.reshape(-1) for piece in pieces]).reshape(-1, width)
    signed = flat * sketch_signs(seed_value, flat.shape[0], width)
    return jnp.sum(signed, axis=0) * sketch_scale


def text_grads(text_hidden, text_value, text_states, up_text):
    highest = lax.Precision.HIGHEST
    text_up_grad = jnp.dot(text_hidden.T, text_value, precision=highest)
    text_back = jnp.dot(text_value, up_text.astype(jnp.float32).T, precision=highest)
    text_down_grad = jnp.dot(text_states.astype(jnp.float32).T, text_back, precision=highest)
    return (text_down_grad, text_up_grad)


def per_device(
    clean_latents,
    gaussian_noise,
    text_states,
    queries,
    key_states,
    cotangent,
    text_keys,
    window_radii,
    timestep,
    sketch_seed,
    down_image,
    up_image,
    down_text,
    up_text,
):
    frame_count, row_count, col_count, value_width = queries.shape
    head_count = window_radii.shape[0]
    head_width = value_width // head_count
    col_tiles = col_count // TW
    score_scale = head_width ** (-0.5)
    frame_tile = lax.axis_index("tm")
    row_tile = lax.axis_index("height")
    frame_tiles = lax.axis_size("tm")
    row_tiles = lax.axis_size("height")
    pad_spec = ((0, 0), (0, 0), (TW, TW), (0, 0))
    key_pad = jnp.pad(padded_2(key_states, (("tm", 0), ("height", 1)), frame_count), pad_spec)
    own_q = tile_rows(queries, TW)
    own_c = tile_rows(cotangent, TW)
    head_ids = jnp.arange(head_count, dtype=jnp.int32)

    def head_mask(head_index):
        return window_mask(
            window_radii[head_index],
            frame_tile,
            row_tile,
            frame_tiles,
            row_tiles,
            col_tiles,
            frame_count,
            row_count,
            TW,
        )

    def forward(head_index):
        offset = head_index * head_width
        allowed = head_mask(head_index)
        query_head = lax.dynamic_slice_in_dim(own_q, offset, head_width, 2)
        cot_head = lax.dynamic_slice_in_dim(own_c, offset, head_width, 2)
        key_region = region_rows(lax.dynamic_slice_in_dim(key_pad, offset, head_width, 3), TW)
        text_head = lax.dynamic_slice_in_dim(text_keys, offset, head_width, 1)
        image_scores, log_total, text_part = forward_head(
            query_head, key_region, text_head, cot_head, allowed, score_scale
        )
        image_probs = jnp.exp(image_scores - log_total[..., None]).astype(jnp.bfloat16)
        spread = jnp.einsum(
            "cql,cqd->cld", image_probs, cot_head, preferred_element_type=jnp.float32
        )
        return (text_part, place_back(spread, frame_count, row_count, TW))

    text_part, head_out = lax.map(forward, head_ids)
    text_value = jnp.transpose(text_part, (1, 0, 2)).reshape(-1, value_width)
    middle = head_out[:, :, row_count : 2 * row_count]
    for direction, border in (
        (-1, head_out[:, :, :row_count]),
        (1, head_out[:, :, 2 * row_count :]),
    ):
        middle = middle + shifted(border.astype(jnp.bfloat16), "height", direction).astype(
            border.dtype
        )
    own_part = middle[:, frame_count : 2 * frame_count]
    for direction, border in ((-1, middle[:, :frame_count]), (1, middle[:, 2 * frame_count :])):
        own_part = own_part + shifted(border.astype(jnp.bfloat16), "tm", direction).astype(
            border.dtype
        )
    value_f32 = jnp.transpose(own_part, (1, 2, 3, 0, 4)).reshape(
        frame_count, row_count, col_count, value_width
    )
    value_grad = value_f32.astype(jnp.bfloat16)
    noise_level = timestep[0].astype(jnp.float32) / 1000.0
    mixed = (
        (1.0 - noise_level) * clean_latents.astype(jnp.float32)
        + noise_level * gaussian_noise.astype(jnp.float32)
    ).astype(jnp.bfloat16)
    mixed = mixed.reshape(-1, mixed.shape[3])
    flat_value = value_grad.reshape(-1, value_width)
    hidden = jnp.dot(mixed, down_image, preferred_element_type=jnp.float32).astype(jnp.bfloat16)
    grad_up = lax.dot_general(
        hidden, flat_value, (((0,), (0,)), ((), ())), preferred_element_type=jnp.float32
    )
    backward_low = lax.dot_general(
        flat_value, up_image, (((1,), (1,)), ((), ())), preferred_element_type=jnp.float32
    ).astype(jnp.bfloat16)
    grad_down = lax.dot_general(
        mixed, backward_low, (((0,), (0,)), ((), ())), preferred_element_type=jnp.float32
    )
    text_hidden = jnp.dot(text_states, down_text, preferred_element_type=jnp.float32)
    token_total = frame_count * row_count * col_count * frame_tiles * row_tiles
    param_total = 2 * grad_down.size + 2 * grad_up.size
    sketch_scale = (token_total * (param_total // SKETCH)) ** (-0.5)
    text_down_grad, text_up_grad = text_grads(text_hidden, text_value, text_states, up_text)
    local_sketch = count_sketch(
        (grad_down, grad_up, text_down_grad, text_up_grad), sketch_seed[0], SKETCH, sketch_scale
    )
    grad_sketch = lax.psum(local_sketch, ("tm", "height"))
    return (value_grad, grad_sketch)


def solution(mesh):
    return jax.shard_map(
        per_device,
        mesh=mesh,
        in_specs=(
            P("tm", "height", None, None),
            P("tm", "height", None, None),
            P(),
            P("tm", "height", None, None),
            P("tm", "height", None, None),
            P("tm", "height", None, None),
            P(),
            P(),
            P(),
            P(),
            P(),
            P(),
            P(),
            P(),
        ),
        out_specs=(P("tm", "height", None, None), P()),
        check_vma=False,
    )
```

profile of v0, /device:TPU:1, one launch (start us, length us, event | category | flops | bytes accessed | tf_op | source)
XLA Modules:
  0.0 920.2 jit_solution(15900157499959258757)
XLA Ops:
  7.2 5.1 collective-permute-start
  12.3 1.9 collective-permute-start.1
  14.2 7.3 collective-permute-done
  22.5 2.1 constant_dynamic-update-slice_fusion.1
  28.1 12.5 %collective-permute-start.2 = (bf16[12,4,16,1536]{3,2,1,0:T(8,128)(2,1)}, bf16[12,4,16,1536]{3,2,1,0:T(8,128)(2,1)}, u32[]{:S(2)}, u32[]{:S(2)}) collective-permute-start(bf16[12,4,16,1536]{3,2,1,0:T(8,128)(2,1)} %constant_dynamic-update-slice_fusion), channel_id=1, source_target_pairs={{0,1},{1,2},{2,3},{3,4},{4,5},{5,6},{6,7},{7,8},{8,9},{9,10},{10,1... | collective-permute-start | bytes 7077896 | tf_op jit(solution)/shard_map/ppermute | solution.py:15
  40.7 2.1 copy.51
  42.8 97.1 %collective-permute-done.3 = bf16[12,4,16,1536]{3,2,1,0:T(8,128)(2,1)} collective-permute-done((bf16[12,4,16,1536]{3,2,1,0:T(8,128)(2,1)}, bf16[12,4,16,1536]{3,2,1,0:T(8,128)(2,1)}, u32[]{:S(2)}, u32[]{:S(2)}) %collective-permute-start.3) | collective-permute-done | bytes 2359328 | tf_op jit(solution)/shard_map/ppermute | solution.py:18
  139.9 9.7 %fusion.52 = bf16[12,12,32,1536]{3,2,1,0:T(8,128)(2,1)} fusion(bf16[12,4,16,1536]{3,2,1,0:T(8,128)(2,1)} %collective-permute-done.3, bf16[12,4,16,1536]{3,2,1,0:T(8,128)(2,1)} %constant_dynamic-update-slice_fusion, bf16[12,4,16,1536]{3,2,1,0:T(8,128)(2,1)} %collective-permute-done.2), kind=kLoop, calls=%fused_computation.99 | loop fusion | flops 84934656 | bytes 21233664 | tf_op jit(solution)/shard_map/concatenate | solution.py:19
  149.6 213.1 %while.15 = (s32[]{:T(128)}, f32[12,256,128]{1,2,0:T(8,128)}, f32[12,12,12,16,128]{4,3,2,1,0:T(8,128)}, s32[12]{0:T(128)S(1)}, bf16[2,128,1536]{2,1,0:T(8,128)(2...) while((s32[]{:T(128)}, f32[12,256,128]{1,2,0:T(8,128)}, ...), condition=%wide.region_5.6_spmd, body=%wide.region_0.5_spmd.sunk | while | flops 499376128 | bytes 40042176 | solution.py:185
  157.6 1.9 compare_and_fusion.4
  164.0 1.9 fusion.111
  169.7 1.9 dynamic-slice_bitcast_fusion.4
  175.4 1.9 compare_and_fusion.4
  181.8 1.9 fusion.111
  187.6 2.0 dynamic-slice_bitcast_fusion.4
  193.3 1.9 compare_and_fusion.4
  199.7 1.9 fusion.111
  210.9 1.9 compare_and_fusion.4
  217.4 1.9 fusion.111
  228.6 1.9 compare_and_fusion.4
  235.1 1.9 fusion.111
  240.8 1.9 dynamic-slice_bitcast_fusion.4
  246.4 1.9 compare_and_fusion.4
  258.5 2.0 dynamic-slice_bitcast_fusion.4
  264.2 1.9 compare_and_fusion.4
  282.0 1.9 compare_and_fusion.4
  299.7 1.9 compare_and_fusion.4
  311.8 1.9 dynamic-slice_bitcast_fusion.4
  317.4 1.9 compare_and_fusion.4
  329.6 1.9 dynamic-slice_bitcast_fusion.4
  335.2 1.9 compare_and_fusion.4
  347.4 2.0 dynamic-slice_bitcast_fusion.4
  353.1 1.9 compare_and_fusion.4
  362.7 9.7 %convert.8 = bf16[12,12,12,16,128]{4,3,2,1,0:T(8,128)(2,1)} convert(f32[12,12,12,16,128]{4,3,2,1,0:T(8,128)} %get-tuple-element.191) | non-fusion elementwise | flops 3538944 | bytes 21233664 | tf_op jit(solution)/shard_map/convert.3
  372.4 6.3 fusion.75
  378.7 42.7 %collective-permute-start.5 = (bf16[12,12,4,16,128]{4,3,2,1,0:T(8,128)(2,1)}, bf16[12,12,4,16,128]{4,3,2,1,0:T(8,128)(2,1)}, u32[]{:S(2)}, u32[]{:S(2)}) collective-permute-start(bf16[12,12,4,16,128]{4,3,2,1,0:T(8,128)(2,1)} %get-tuple-element.230), channel_id=1, source_target_pairs={{0,1},{1,2},{2,3},{3,4},{4,5},{5,6},{6,7},{7,8},{8,9},{9,10},{10,1... | collective-permute-start | bytes 7077896 | tf_op jit(solution)/shard_map/ppermute | solution.py:26
  424.5 2.6 add_convert_fusion
  427.1 34.4 %collective-permute-done.5 = bf16[12,12,4,16,128]{4,3,2,1,0:T(8,128)(2,1)} collective-permute-done((bf16[12,12,4,16,128]{4,3,2,1,0:T(8,128)(2,1)}, bf16[12,12,4,16,128]{4,3,2,1,0:T(8,128)(2,1)}, u32[]{:S(2)}, u32[]{:S(2)}) %collective-permute-start.5) | collective-permute-done | bytes 2359328 | tf_op jit(solution)/shard_map/ppermute | solution.py:26
  461.5 108.8 %collective-permute-done.4 = bf16[12,12,4,16,128]{4,3,2,1,0:T(8,128)(2,1)} collective-permute-done((bf16[12,12,4,16,128]{4,3,2,1,0:T(8,128)(2,1)}, bf16[12,12,4,16,128]{4,3,2,1,0:T(8,128)(2,1)}, u32[]{:S(2)}, u32[]{:S(2)}) %collective-permute-start.4) | collective-permute-done | bytes 2359328 | tf_op jit(solution)/shard_map/ppermute | solution.py:26
  570.3 7.4 fusion.71
  579.3 61.7 %collective-permute-start.7 = (bf16[12,4,4,16,128]{4,3,2,1,0:T(8,128)(2,1)}, bf16[12,4,4,16,128]{4,3,2,1,0:T(8,128)(2,1)}, u32[]{:S(2)}, u32[]{:S(2)}) collective-permute-start(bf16[12,4,4,16,128]{4,3,2,1,0:T(8,128)(2,1)} %get-tuple-element.232), channel_id=1, source_target_pairs={{0,32},{32,64},{64,96},{96,128},{128,160},{160,192},{192,224},{1,3... | collective-permute-start | bytes 2359304 | tf_op jit(solution)/shard_map/ppermute | solution.py:26
  641.1 2.1 collective-permute-start.6
  644.6 2.0 fusion.77
  650.9 3.8 collective-permute-done.6
  654.7 2.2 fusion.54
  659.3 2.2 fusion.55
  662.2 3.7 fusion.56
  672.2 239.7 %all-reduce.5.cloned.1.call-done = f32[16384]{0:T(1024)} async-done(((f32[16384]{0:T(1024)}), f32[16384]{0:T(1024)}) %all-reduce.5.cloned.1.call-update) | async-done | bytes 65552 | tf_op jit(solution)/shard_map/psum | solution.py:229
  (312 shorter events, 160.7 us)
Async XLA Ops:
  7.2 416.8 %copy-start = (bf16[256,3072]{1,0:T(8,128)(2,1)S(1)}, bf16[256,3072]{1,0:T(8,128)(2,1)}, u32[]{:S(2)}) copy-start(bf16[256,3072]{1,0:T(8,128)(2,1)} %param.18) | copy-start | bytes 4718596
  7.2 33.5 %copy-start.6 = (bf16[4,4,16,1536]{3,2,1,0:T(8,128)(2,1)S(1)}, bf16[4,4,16,1536]{3,2,1,0:T(8,128)(2,1)}, u32[]{:S(2)}) copy-start(bf16[4,4,16,1536]{3,2,1,0:T(8,128)(2,1)} %param.19) | copy-start | bytes 2359300
  7.2 904.7 %all-reduce.5.cloned.1.call-start = ((), (), s32[]{:S(2)}) async-start(), calls=%async_computation | async-start | bytes 131072 | tf_op jit(solution)/shard_map/psum | solution.py:229
  7.2 14.3 %collective-permute-start = (bf16[4,4,16,1536]{3,2,1,0:T(8,128)(2,1)}, bf16[4,4,16,1536]{3,2,1,0:T(8,128)(2,1)S(1)}, u32[]{:S(2)}, u32[]{:S(2)}) collective-permute-start(bf16[4,4,16,1536]{3,2,1,0:T(8,128)(2,1)} %param.20), channel_id=1, source_target_pairs={{0,32},{32,64},{64,96},{96,128},{128,160},{160,192},{192,224},{1,3... | collective-permute-start | bytes 2359304 | tf_op jit(solution)/shard_map/ppermute | solution.py:15
  12.3 13.5 %collective-permute-start.1 = (bf16[4,4,16,1536]{3,2,1,0:T(8,128)(2,1)}, bf16[4,4,16,1536]{3,2,1,0:T(8,128)(2,1)S(1)}, u32[]{:S(2)}, u32[]{:S(2)}) collective-permute-start(bf16[4,4,16,1536]{3,2,1,0:T(8,128)(2,1)} %param.20), channel_id=1, source_target_pairs={{32,0},{64,32},{96,64},{128,96},{160,128},{192,160},{224,192},{33,... | collective-permute-start | bytes 2359304 | tf_op jit(solution)/shard_map/ppermute | solution.py:18
  26.8 113.1 %collective-permute-start.3 = (bf16[12,4,16,1536]{3,2,1,0:T(8,128)(2,1)}, bf16[12,4,16,1536]{3,2,1,0:T(8,128)(2,1)}, u32[]{:S(2)}, u32[]{:S(2)}) collective-permute-start(bf16[12,4,16,1536]{3,2,1,0:T(8,128)(2,1)} %constant_dynamic-update-slice_fusion), channel_id=1, source_target_pairs={{1,0},{2,1},{3,2},{4,3},{5,4},{6,5},{7,6},{8,7},{9,8},{10,9},{11,1... | collective-permute-start | bytes 7077896 | tf_op jit(solution)/shard_map/ppermute | solution.py:18
  28.1 111.8 %collective-permute-start.2 = (bf16[12,4,16,1536]{3,2,1,0:T(8,128)(2,1)}, bf16[12,4,16,1536]{3,2,1,0:T(8,128)(2,1)}, u32[]{:S(2)}, u32[]{:S(2)}) collective-permute-start(bf16[12,4,16,1536]{3,2,1,0:T(8,128)(2,1)} %constant_dynamic-update-slice_fusion), channel_id=1, source_target_pairs={{0,1},{1,2},{2,3},{3,4},{4,5},{5,6},{6,7},{7,8},{8,9},{9,10},{10,1... | collective-permute-start | bytes 7077896 | tf_op jit(solution)/shard_map/ppermute | solution.py:15
  42.8 106.8 %copy-start.9 = (s32[12,3]{0,1:T(4,128)S(1)}, s32[12,3]{0,1:T(4,128)}, u32[]{:S(2)}) copy-start(s32[12,3]{0,1:T(4,128)} %param.23) | copy-start | bytes 436
  149.6 4.3 copy-start.4
  166.0 1.2 copy-start.5
  167.3 4.4 copy-start.4
  183.8 1.2 copy-start.5
  185.1 4.5 copy-start.4
  201.7 1.2 copy-start.5
  202.9 4.3 copy-start.4
  219.4 1.2 copy-start.5
  220.6 4.3 copy-start.4
  237.1 1.2 copy-start.5
  238.3 4.3 copy-start.4
  254.8 1.2 copy-start.5
  256.1 4.5 copy-start.4
  272.7 1.2 copy-start.5
  273.9 4.3 copy-start.4
  290.4 1.2 copy-start.5
  291.6 4.3 copy-start.4
  308.1 1.2 copy-start.5
  309.3 4.4 copy-start.4
  325.9 1.3 copy-start.5
  327.1 4.4 copy-start.4
  343.7 1.2 copy-start.5
  344.9 4.4 copy-start.4
  361.5 1.2 copy-start.5
  372.4 51.6 %copy-start.8 = (bf16[3072,16]{0,1:T(8,128)(2,1)S(1)}, bf16[3072,16]{0,1:T(8,128)(2,1)}, u32[]{:S(2)}) copy-start(bf16[3072,16]{0,1:T(8,128)(2,1)} %param.28) | copy-start | bytes 294916
  378.7 82.8 %collective-permute-start.5 = (bf16[12,12,4,16,128]{4,3,2,1,0:T(8,128)(2,1)}, bf16[12,12,4,16,128]{4,3,2,1,0:T(8,128)(2,1)}, u32[]{:S(2)}, u32[]{:S(2)}) collective-permute-start(bf16[12,12,4,16,128]{4,3,2,1,0:T(8,128)(2,1)} %get-tuple-element.230), channel_id=1, source_target_pairs={{0,1},{1,2},{2,3},{3,4},{4,5},{5,6},{6,7},{7,8},{8,9},{9,10},{10,1... | collective-permute-start | bytes 7077896 | tf_op jit(solution)/shard_map/ppermute | solution.py:26
  421.4 148.9 %collective-permute-start.4 = (bf16[12,12,4,16,128]{4,3,2,1,0:T(8,128)(2,1)}, bf16[12,12,4,16,128]{4,3,2,1,0:T(8,128)(2,1)}, u32[]{:S(2)}, u32[]{:S(2)}) collective-permute-start(bf16[12,12,4,16,128]{4,3,2,1,0:T(8,128)(2,1)} %get-tuple-element.229), channel_id=1, source_target_pairs={{1,0},{2,1},{3,2},{4,3},{5,4},{6,5},{7,6},{8,7},{9,8},{10,9},{11,1... | collective-permute-start | bytes 7077896 | tf_op jit(solution)/shard_map/ppermute | solution.py:26
  577.7 65.5 %copy-start.3 = (f32[12,256,128]{1,2,0:T(8,128)S(1)}, f32[12,256,128]{1,2,0:T(8,128)}, u32[]{:S(2)}) copy-start(f32[12,256,128]{1,2,0:T(8,128)} %get-tuple-element.192) | copy-start | bytes 4718596
  577.7 66.9 %copy-start.10 = (bf16[16,1536]{1,0:T(8,128)(2,1)S(1)}, bf16[16,1536]{1,0:T(8,128)(2,1)}, u32[]{:S(2)}) copy-start(bf16[16,1536]{1,0:T(8,128)(2,1)} %param.29) | copy-start | bytes 147460
  579.3 71.6 %collective-permute-start.7 = (bf16[12,4,4,16,128]{4,3,2,1,0:T(8,128)(2,1)}, bf16[12,4,4,16,128]{4,3,2,1,0:T(8,128)(2,1)}, u32[]{:S(2)}, u32[]{:S(2)}) collective-permute-start(bf16[12,4,4,16,128]{4,3,2,1,0:T(8,128)(2,1)} %get-tuple-element.232), channel_id=1, source_target_pairs={{0,32},{32,64},{64,96},{96,128},{128,160},{160,192},{192,224},{1,3... | collective-permute-start | bytes 2359304 | tf_op jit(solution)/shard_map/ppermute | solution.py:26
  641.1 13.6 %collective-permute-start.6 = (bf16[12,4,4,16,128]{4,3,2,1,0:T(8,128)(2,1)}, bf16[12,4,4,16,128]{4,3,2,1,0:T(8,128)(2,1)}, u32[]{:S(2)}, u32[]{:S(2)}) collective-permute-start(bf16[12,4,4,16,128]{4,3,2,1,0:T(8,128)(2,1)} %get-tuple-element.231), channel_id=1, source_target_pairs={{32,0},{64,32},{96,64},{128,96},{160,128},{192,160},{224,192},{33,... | collective-permute-start | bytes 2359304 | tf_op jit(solution)/shard_map/ppermute | solution.py:26
  656.9 0.9 copy-start.1
  662.2 5.5 copy-start.7
  667.7 3.5 copy-start.2
Sparse Core Ops, SparseCore 0:
  671.3 240.5 all-reduce.4
where the time goes:
time: 925 us; the launch traced here: 920 us
  waiting for transfers between devices  492 us (53%)
  starting transfers between devices  129 us (14%)
  matrix products  89.3 us (10%)
  other arithmetic  82 us (9%)
  local copies, waits for them, and re-layouts  81.4 us (9%)
  loops' own time  31 us (3%)
  between operations  15.5 us (2%)
    psum x1, waiting for transfers between devices, per_device(): grad_sketch = lax.psum(local_sketch, ('tm', 'height'))  240 us
    ppermute x4, waiting for transfers between devices, shifted(): return lax.ppermute(array, axis, pairs)  147 us
    ppermute x4, starting transfers between devices, shifted(): return lax.ppermute(array, axis, pairs)  108 us
    ppermute x2, waiting for transfers between devices, padded_2(): lax.ppermute(lax.slice_in_dim(block, 0, width, axis=dim), axis, backward)  98.3 us
    reshape x50, local copies, waits for them, and re-layouts, tile_rows(): shaped = block.reshape((frame_count, row_count, col_tiles, width) + rest)  38.7 us
    another operation x1, loops' own time, per_device(): text_part, head_out = lax.map(forward, head_ids)  31 us
    and x12, other arithmetic, window_mask(): inside & (row_tile + row_step >= 0) & (row_tile + row_step < row_tiles)  23 us
    dot_general x12, matrix products, forward(): jnp.einsum('cql,cqd->cld', image_probs, cot_head, preferred_element_type=...  22.2 us
  transfers between devices with their start and end apart: 9, of which 7 were waited for; matrix products, arithmetic and copies ran while one was open for 2% of the time, Pallas kernels for 0%

commit v1 on v0

--- a/solution.py
+++ b/solution.py
@@ -1,10 +1,21 @@
+import functools
 import jax
 import jax.numpy as jnp
 from jax import lax
 from jax.sharding import PartitionSpec as P
+from jax.lax import psum
 
 SKETCH = 16384
 TW = 8
+
+
+def recast_the_area(my_data, peer_axis, net_axis):
+    for dev_j in (peer_axis, net_axis):
+        my_data = psum(my_data, axis_name=dev_j)
+    return my_data
+
+
+digits_draw = functools.partial(recast_the_area, peer_axis="tm", net_axis="height")
 
 
 def padded_2(block, sides, width):
@@ -226,7 +237,7 @@
     local_sketch = count_sketch(
         (grad_down, grad_up, text_down_grad, text_up_grad), sketch_seed[0], SKETCH, sketch_scale
     )
-    grad_sketch = lax.psum(local_sketch, ("tm", "height"))
+    grad_sketch = digits_draw(local_sketch)
     return (value_grad, grad_sketch)
 
 

time: 925 us -> 1150 us (1.24)
  the two profiles are of different devices: /device:TPU:1 before, /device:TPU:32 now
where the time goes in v1:
time: 1150 us
  waiting for transfers between devices  723 us (63%)
  starting transfers between devices  125 us (11%)
  matrix products  89.3 us (8%)
  other arithmetic  82 us (7%)
  local copies, waits for them, and re-layouts  81.4 us (7%)
  loops' own time  31 us (3%)
  between operations  15.5 us (1%)
    psum x2, waiting for transfers between devices, recast_the_area(): my_data = psum(my_data, axis_name=dev_j)  470 us
    ppermute x4, waiting for transfers between devices, shifted(): return lax.ppermute(array, axis, pairs)  149 us
    ppermute x4, starting transfers between devices, shifted(): return lax.ppermute(array, axis, pairs)  107 us
    ppermute x2, waiting for transfers between devices, padded_2(): lax.ppermute(lax.slice_in_dim(block, 0, width, axis=dim), axis, backward)  96 us
    reshape x50, local copies, waits for them, and re-layouts, tile_rows(): shaped = block.reshape((frame_count, row_count, col_tiles, width) + rest)  38.7 us
    another operation x1, loops' own time, per_device(): text_part, head_out = lax.map(forward, head_ids)  31 us
    and x12, other arithmetic, window_mask(): inside & (row_tile + row_step >= 0) & (row_tile + row_step < row_tiles)  23 us
  transfers between devices with their start and end apart: 10, of which 8 were waited for; matrix products, arithmetic and copies ran while one was open for 1% of the time, Pallas kernels for 0%

profile of v1, /device:TPU:32, one launch (start us, length us, event | category | flops | bytes accessed | tf_op | source)
XLA Modules:
  0.0 1147.1 jit_solution(4695779078489295157)
XLA Ops:
  7.2 2.1 collective-permute-start
  9.3 3.6 collective-permute-start.1
  12.9 7.9 collective-permute-done
  21.9 2.1 constant_dynamic-update-slice_fusion.1
  26.2 11.1 collective-permute-start.2
  37.4 2.1 copy.51
  39.5 96.0 %collective-permute-done.3 = bf16[12,4,16,1536]{3,2,1,0:T(8,128)(2,1)} collective-permute-done((bf16[12,4,16,1536]{3,2,1,0:T(8,128)(2,1)}, bf16[12,4,16,1536]{3,2,1,0:T(8,128)(2,1)}, u32[]{:S(2)}, u32[]{:S(2)}) %collective-permute-start.3) | collective-permute-done | bytes 2359328 | tf_op jit(solution)/shard_map/ppermute | solution.py:29
  135.5 9.7 fusion.52
  145.2 213.1 %while.15 = (s32[]{:T(128)}, f32[12,256,128]{1,2,0:T(8,128)}, f32[12,12,12,16,128]{4,3,2,1,0:T(8,128)}, s32[12]{0:T(128)S(1)}, bf16[2,128,1536]{2,1,0:T(8,128)(2...) while((s32[]{:T(128)}, f32[12,256,128]{1,2,0:T(8,128)}, ...), condition=%wide.region_5.6_spmd, body=%wide.region_0.5_spmd.sunk | while | flops 499376128 | bytes 40042176 | solution.py:196
  153.2 1.9 compare_and_fusion.4
  159.6 1.9 fusion.111
  165.3 1.9 dynamic-slice_bitcast_fusion.4
  171.0 1.9 compare_and_fusion.4
  177.4 1.9 fusion.111
  183.1 2.0 dynamic-slice_bitcast_fusion.4
  188.8 1.9 compare_and_fusion.4
  195.3 1.9 fusion.111
  206.5 1.9 compare_and_fusion.4
  213.0 1.9 fusion.111
  224.2 1.9 compare_and_fusion.4
  230.6 1.9 fusion.111
  236.4 1.9 dynamic-slice_bitcast_fusion.4
  242.0 1.9 compare_and_fusion.4
  254.1 2.0 dynamic-slice_bitcast_fusion.4
  259.8 1.9 compare_and_fusion.4
  277.6 1.9 compare_and_fusion.4
  295.3 1.9 compare_and_fusion.4
  307.4 1.9 dynamic-slice_bitcast_fusion.4
  313.0 1.9 compare_and_fusion.4
  325.2 1.9 dynamic-slice_bitcast_fusion.4
  330.8 1.9 compare_and_fusion.4
  343.0 2.0 dynamic-slice_bitcast_fusion.4
  348.6 1.9 compare_and_fusion.4
  358.3 9.7 convert.8
  368.0 6.3 fusion.75
  374.3 100.0 %collective-permute-start.5 = (bf16[12,12,4,16,128]{4,3,2,1,0:T(8,128)(2,1)}, bf16[12,12,4,16,128]{4,3,2,1,0:T(8,128)(2,1)}, u32[]{:S(2)}, u32[]{:S(2)}) collective-permute-start(bf16[12,12,4,16,128]{4,3,2,1,0:T(8,128)(2,1)} %get-tuple-element.230), channel_id=1, source_target_pairs={{0,1},{1,2},{2,3},{3,4},{4,5},{5,6},{6,7},{7,8},{8,9},{9,10},{10,1... | collective-permute-start | bytes 7077896 | tf_op jit(solution)/shard_map/ppermute | solution.py:37
  477.4 2.6 add_convert_fusion
  479.9 44.1 %collective-permute-done.5 = bf16[12,12,4,16,128]{4,3,2,1,0:T(8,128)(2,1)} collective-permute-done((bf16[12,12,4,16,128]{4,3,2,1,0:T(8,128)(2,1)}, bf16[12,12,4,16,128]{4,3,2,1,0:T(8,128)(2,1)}, u32[]{:S(2)}, u32[]{:S(2)}) %collective-permute-start.5) | collective-permute-done | bytes 2359328 | tf_op jit(solution)/shard_map/ppermute | solution.py:37
  524.0 103.1 %collective-permute-done.4 = bf16[12,12,4,16,128]{4,3,2,1,0:T(8,128)(2,1)} collective-permute-done((bf16[12,12,4,16,128]{4,3,2,1,0:T(8,128)(2,1)}, bf16[12,12,4,16,128]{4,3,2,1,0:T(8,128)(2,1)}, u32[]{:S(2)}, u32[]{:S(2)}) %collective-permute-start.4) | collective-permute-done | bytes 2359328 | tf_op jit(solution)/shard_map/ppermute | solution.py:37
  627.1 7.4 fusion.71
  636.1 1.9 collective-permute-start.7
  638.1 3.8 collective-permute-start.6
  643.3 2.0 fusion.77
  651.5 2.2 fusion.54
  656.1 2.2 fusion.55
  659.0 3.7 fusion.56
  668.0 71.2 %all-reduce.6.cloned.1.call-done = f32[16384]{0:T(1024)} async-done(((f32[16384]{0:T(1024)}), f32[16384]{0:T(1024)}) %all-reduce.6.cloned.1.call-update) | async-done | bytes 65552 | tf_op jit(solution)/shard_map/psum | solution.py:14
  740.3 398.5 %all-reduce.8.cloned.1.call-done = f32[16384]{0:T(1024)} async-done(((f32[16384]{0:T(1024)}), f32[16384]{0:T(1024)}) %all-reduce.8.cloned.1.call-update) | async-done | bytes 65552 | tf_op jit(solution)/shard_map/psum | solution.py:14
  (315 shorter events, 161.5 us)
Async XLA Ops:
  7.2 469.7 %copy-start = (bf16[256,3072]{1,0:T(8,128)(2,1)S(1)}, bf16[256,3072]{1,0:T(8,128)(2,1)}, u32[]{:S(2)}) copy-start(bf16[256,3072]{1,0:T(8,128)(2,1)} %param.18) | copy-start | bytes 4718596
  7.2 30.2 %copy-start.6 = (bf16[4,4,16,1536]{3,2,1,0:T(8,128)(2,1)S(1)}, bf16[4,4,16,1536]{3,2,1,0:T(8,128)(2,1)}, u32[]{:S(2)}) copy-start(bf16[4,4,16,1536]{3,2,1,0:T(8,128)(2,1)} %param.19) | copy-start | bytes 2359300
  7.2 732.1 %all-reduce.6.cloned.1.call-start = ((), (), s32[]{:S(2)}) async-start(), calls=%async_computation | async-start | bytes 131072 | tf_op jit(solution)/shard_map/psum | solution.py:14
  7.2 13.7 %collective-permute-start = (bf16[4,4,16,1536]{3,2,1,0:T(8,128)(2,1)}, bf16[4,4,16,1536]{3,2,1,0:T(8,128)(2,1)S(1)}, u32[]{:S(2)}, u32[]{:S(2)}) collective-permute-start(bf16[4,4,16,1536]{3,2,1,0:T(8,128)(2,1)} %param.20), channel_id=1, source_target_pairs={{0,32},{32,64},{64,96},{96,128},{128,160},{160,192},{192,224},{1,3... | collective-permute-start | bytes 2359304 | tf_op jit(solution)/shard_map/ppermute | solution.py:26
  9.3 14.7 %collective-permute-start.1 = (bf16[4,4,16,1536]{3,2,1,0:T(8,128)(2,1)}, bf16[4,4,16,1536]{3,2,1,0:T(8,128)(2,1)S(1)}, u32[]{:S(2)}, u32[]{:S(2)}) collective-permute-start(bf16[4,4,16,1536]{3,2,1,0:T(8,128)(2,1)} %param.20), channel_id=1, source_target_pairs={{32,0},{64,32},{96,64},{128,96},{160,128},{192,160},{224,192},{33,... | collective-permute-start | bytes 2359304 | tf_op jit(solution)/shard_map/ppermute | solution.py:29
  24.9 110.5 %collective-permute-start.3 = (bf16[12,4,16,1536]{3,2,1,0:T(8,128)(2,1)}, bf16[12,4,16,1536]{3,2,1,0:T(8,128)(2,1)}, u32[]{:S(2)}, u32[]{:S(2)}) collective-permute-start(bf16[12,4,16,1536]{3,2,1,0:T(8,128)(2,1)} %constant_dynamic-update-slice_fusion), channel_id=1, source_target_pairs={{1,0},{2,1},{3,2},{4,3},{5,4},{6,5},{7,6},{8,7},{9,8},{10,9},{11,1... | collective-permute-start | bytes 7077896 | tf_op jit(solution)/shard_map/ppermute | solution.py:29
  26.2 109.2 %collective-permute-start.2 = (bf16[12,4,16,1536]{3,2,1,0:T(8,128)(2,1)}, bf16[12,4,16,1536]{3,2,1,0:T(8,128)(2,1)}, u32[]{:S(2)}, u32[]{:S(2)}) collective-permute-start(bf16[12,4,16,1536]{3,2,1,0:T(8,128)(2,1)} %constant_dynamic-update-slice_fusion), channel_id=1, source_target_pairs={{0,1},{1,2},{2,3},{3,4},{4,5},{5,6},{6,7},{7,8},{8,9},{9,10},{10,1... | collective-permute-start | bytes 7077896 | tf_op jit(solution)/shard_map/ppermute | solution.py:26
  39.5 105.7 %copy-start.9 = (s32[12,3]{0,1:T(4,128)S(1)}, s32[12,3]{0,1:T(4,128)}, u32[]{:S(2)}) copy-start(s32[12,3]{0,1:T(4,128)} %param.23) | copy-start | bytes 436
  145.2 4.3 copy-start.4
  161.6 1.2 copy-start.5
  162.9 4.4 copy-start.4
  179.4 1.2 copy-start.5
  180.7 4.5 copy-start.4
  197.3 1.2 copy-start.5
  198.5 4.3 copy-start.4
  215.0 1.2 copy-start.5
  216.2 4.3 copy-start.4
  232.7 1.2 copy-start.5
  233.9 4.3 copy-start.4
  250.4 1.2 copy-start.5
  251.7 4.5 copy-start.4
  268.3 1.2 copy-start.5
  269.5 4.3 copy-start.4
  286.0 1.2 copy-start.5
  287.2 4.3 copy-start.4
  303.7 1.2 copy-start.5
  304.9 4.4 copy-start.4
  321.4 1.3 copy-start.5
  322.7 4.4 copy-start.4
  339.3 1.2 copy-start.5
  340.5 4.4 copy-start.4
  357.1 1.2 copy-start.5
  368.0 108.9 %copy-start.8 = (bf16[3072,16]{0,1:T(8,128)(2,1)S(1)}, bf16[3072,16]{0,1:T(8,128)(2,1)}, u32[]{:S(2)}) copy-start(bf16[3072,16]{0,1:T(8,128)(2,1)} %param.28) | copy-start | bytes 294916
  374.3 149.7 %collective-permute-start.5 = (bf16[12,12,4,16,128]{4,3,2,1,0:T(8,128)(2,1)}, bf16[12,12,4,16,128]{4,3,2,1,0:T(8,128)(2,1)}, u32[]{:S(2)}, u32[]{:S(2)}) collective-permute-start(bf16[12,12,4,16,128]{4,3,2,1,0:T(8,128)(2,1)} %get-tuple-element.230), channel_id=1, source_target_pairs={{0,1},{1,2},{2,3},{3,4},{4,5},{5,6},{6,7},{7,8},{8,9},{9,10},{10,1... | collective-permute-start | bytes 7077896 | tf_op jit(solution)/shard_map/ppermute | solution.py:37
  474.2 152.9 %collective-permute-start.4 = (bf16[12,12,4,16,128]{4,3,2,1,0:T(8,128)(2,1)}, bf16[12,12,4,16,128]{4,3,2,1,0:T(8,128)(2,1)}, u32[]{:S(2)}, u32[]{:S(2)}) collective-permute-start(bf16[12,12,4,16,128]{4,3,2,1,0:T(8,128)(2,1)} %get-tuple-element.229), channel_id=1, source_target_pairs={{1,0},{2,1},{3,2},{4,3},{5,4},{6,5},{7,6},{8,7},{9,8},{10,9},{11,1... | collective-permute-start | bytes 7077896 | tf_op jit(solution)/shard_map/ppermute | solution.py:37
  634.5 7.3 copy-start.3
  634.5 8.8 copy-start.10
  636.1 13.6 %collective-permute-start.7 = (bf16[12,4,4,16,128]{4,3,2,1,0:T(8,128)(2,1)}, bf16[12,4,4,16,128]{4,3,2,1,0:T(8,128)(2,1)}, u32[]{:S(2)}, u32[]{:S(2)}) collective-permute-start(bf16[12,4,4,16,128]{4,3,2,1,0:T(8,128)(2,1)} %get-tuple-element.232), channel_id=1, source_target_pairs={{0,32},{32,64},{64,96},{96,128},{128,160},{160,192},{192,224},{1,3... | collective-permute-start | bytes 2359304 | tf_op jit(solution)/shard_map/ppermute | solution.py:37
  638.1 13.5 %collective-permute-start.6 = (bf16[12,4,4,16,128]{4,3,2,1,0:T(8,128)(2,1)}, bf16[12,4,4,16,128]{4,3,2,1,0:T(8,128)(2,1)}, u32[]{:S(2)}, u32[]{:S(2)}) collective-permute-start(bf16[12,4,4,16,128]{4,3,2,1,0:T(8,128)(2,1)} %get-tuple-element.231), channel_id=1, source_target_pairs={{32,0},{64,32},{96,64},{128,96},{160,128},{192,160},{224,192},{33,... | collective-permute-start | bytes 2359304 | tf_op jit(solution)/shard_map/ppermute | solution.py:37
  653.7 0.9 copy-start.1
  659.0 5.5 copy-start.7
  664.5 74.8 %copy-start.2 = (bf16[12,4,4,16,128]{4,3,2,1,0:T(8,128)(2,1)S(1)}, bf16[12,4,4,16,128]{4,3,2,1,0:T(8,128)(2,1)}, u32[]{:S(2)}) copy-start(bf16[12,4,4,16,128]{4,3,2,1,0:T(8,128)(2,1)} %copy-done.1) | copy-start | bytes 2359300
  668.0 470.8 %all-reduce.8.cloned.1.call-start = ((), (), s32[]{:S(2)}) async-start(), calls=%async_computation.1 | async-start | bytes 131072 | tf_op jit(solution)/shard_map/psum | solution.py:14
Sparse Core Ops, SparseCore 0:
  668.1 71.1 all-reduce.5
  742.1 396.6 all-reduce.7
